TPU v7x, 256 devices: a whole 4x4x8 slice. The times are simulated.
256 devices in a mesh: ctx: 16 (over x_lo, z), head: 4 (over y), dp: 4 (over x_hi, core).
Axes of the slice: x: 4 (x_hi: 2, x_lo: 2; x = x_hi * 2 + x_lo), y: 4, z: 8, core: 2. Of those that a mesh axis runs over, the one named last changes fastest.
Arguments:
- qkv: bfloat16 [3, 10240, 2560], P(None, ('dp', 'ctx'), 'head'), parts along dimension 1, may hold values from -200 to 200
- tangent: bfloat16 [3, 10240, 2560], P(None, ('dp', 'ctx'), 'head'), parts along dimension 1, may hold values from -6 to 6
- segments: int32 [10240], P(('dp', 'ctx')), parts along dimension 0, may hold values from 0 to 3, never falling along the last dimension, each value on 1 to 1600 neighbouring positions
- out_weight: bfloat16 [2560, 5120], P('head', 'ctx'), may hold values from -0.625 to 0.625
Outputs:
- output: bfloat16 [10240, 5120], P(('dp', 'ctx'), 'head'), parts along dimension 0
- output_tangent: bfloat16 [10240, 5120], P(('dp', 'ctx'), 'head'), parts along dimension 0
There are 4 independent parts, one for each index of `dp`. A program takes and returns all parts, laid end to end along the dimension named above; an argument that names none is the same for every part. Nothing has to cross between parts.
Inputs may be any that keep to these rules, and one draw needn't show every extreme that they name: `segments`: numbers never fall along the sample; every number of 0 to 3 occurs; one video holds exactly 1600 tokens and none more.
All inputs are finite; a program needn't handle non-finite values.
Results may differ from a plain program's by a relative error of at most 0.017.
Values may be sent and summed in bfloat16 or wider, within the bound.
A program may use at most 64 MiB of HBM per device.

v0:
```python
import functools
import math

import jax
import jax.numpy as jnp
from jax import lax
from jax.experimental import pallas as pl
from jax.experimental.pallas import tpu as pltpu
from jax.sharding import PartitionSpec as P

HD = 128
HEADS = 5
BLOCKS = 16
ROWS = 160
SEQ = BLOCKS * ROWS
SLOTS = 6
SEGS = 4
TILE = 512
PART = 480


def several(kind, first, last):
    return [(kind, turn) for turn in range(first, last)]


ORDERS = (
    several("X", 0, 1) + several("K", 0, 2) + several("X", 1, 3) + several("K", 2, 4) + several("D", 0, 2)
    + several("X", 3, 4) + several("D", 2, 5) + several("I", 0, 4) + several("D", 5, 8) + several("R", 0, 8),
    several("O", 0, 4),
    several("F", 0, 4),
    [],
)
KTILES = SEQ // TILE
MESH = pl.DeviceIdType.MESH


def role_of(x_lo, core):
    return x_lo * 2 + core


def chunk_of(block):
    return (block >= 6).astype(jnp.int32) + (block >= 11).astype(jnp.int32)


def chunk_start(chunk):
    return chunk * 5 + jnp.minimum(chunk, 1)


def work_of(x_lo, z, core):
    role = role_of(x_lo, core)
    first = jnp.where(role == 3, 4 * (z // 2), chunk_start(role))
    count = jnp.where(role == 3, 4, 5 + (role == 0).astype(jnp.int32))
    return first, count


def worker_of(head, block, core):
    if head == HEADS - 1:
        return 1, 2 * (block // 4) + core, 1
    role = chunk_of(block)
    return role // 2, 2 * head + core, lax.rem(role, 2)


def fold(op, values):
    parts = [values[:, i:i + 128] for i in range(0, values.shape[1], 128)]
    while len(parts) > 1:
        parts = [op(a, b) for a, b in zip(parts[0::2], parts[1::2])]
    return parts[0]


def signal_if(condition, semaphore, device):
    @pl.when(condition)
    def _():
        pl.semaphore_signal(semaphore, inc=1, device_id=device, device_id_type=MESH)


class Both:
    def __init__(self, copies):
        self.copies = copies

    def start(self):
        for copy in self.copies:
            copy.start()

    def wait_send(self):
        for copy in self.copies:
            copy.wait_send()


class Weights:
    def __init__(self, shard_ref, tail_ref, main_ref, packed_ref, local_sems, *sems):
        self.shard, self.tail, self.local_sems = shard_ref, tail_ref, local_sems
        self.main, self.packed = main_ref, packed_ref
        (self.y_send, self.y_recv, self.z_send, self.z_recv,
         self.x_send, self.x_recv, self.c_send, self.c_recv) = sems
        self.ctx, self.y, dp = lax.axis_index("ctx"), lax.axis_index("head"), lax.axis_index("dp")
        self.x_lo, self.z = self.ctx // 8, lax.rem(self.ctx, 8)
        self.x_hi, self.core = dp // 2, lax.rem(dp, 2)
        self.x = self.x_hi * 2 + self.x_lo
        self.inner = self.x_hi * 2 + 1 - self.x_lo
        self.outer = lax.rem(self.x + 3 + 2 * self.x_lo, 4)
        self.far = lax.rem(self.x + 2, 4)
        self.active = lax.rem(self.z, 2) == self.core
        self.parity = lax.rem(self.z // 4 + self.y, 2)

    def prepare(self):
        for quarter in range(4):
            for side in range(2):
                row = quarter * 160 + side * 80
                self.tail[quarter * 80:(quarter + 1) * 80, side * 64:(side + 1) * 64] = (
                    self.shard[row:row + 80, 256:320]
                )

    def device(self, x=None, z=None, y=None, core=None):
        x = self.x if x is None else x
        z = self.z if z is None else z
        y = self.y if y is None else y
        core = self.core if core is None else core
        return {"ctx": lax.rem(x, 2) * 8 + z, "head": y, "dp": (x // 2) * 2 + core}

    def first_target(self, same):
        y = self.x_lo * 2 + self.z // 4
        x = self.x if same else self.x_hi * 2 + 1 - self.x_lo
        z = lax.rem(self.z + 4 * lax.rem(self.y, 2), 8)
        is_me = (x == self.x) & (y == self.y) & (z == self.z)
        return x, z, y, is_me

    def first_source(self, half):
        y = 2 * half + self.parity
        x = self.x_hi * 2 + self.y // 2
        z = lax.rem(self.z + 4 * self.parity, 8)
        is_me = (x == self.x) & (y == self.y) & (z == self.z)
        return x, z, y, is_me

    def greet(self, barrier):
        for half in range(2):
            x, z, y, is_me = self.first_source(half)
            signal_if(self.active & jnp.logical_not(is_me), barrier, self.device(x, z, y))
        for x in (self.inner, self.outer):
            signal_if(True, barrier, self.device(x=x))
        signal_if(True, barrier, self.device(core=1 - self.core))
        for step in (1, 7):
            signal_if(True, barrier, self.device(z=lax.rem(self.z + step, 8)))

    def greetings(self):
        count = jnp.int32(5)
        for same in (True, False):
            is_me = self.first_target(same)[3]
            count = count + (self.active & jnp.logical_not(is_me)).astype(jnp.int32)
        return count

    def rows(self, quarter):
        return (
            pl.ds(pl.multiple_of(quarter * 160, 160), 160),
            pl.ds(pl.multiple_of(quarter * 80, 80), 80),
        )

    def piece(self, zq, parity, x):
        wide, narrow = self.rows(x)
        return self.main.at[zq, parity, :, wide], self.packed.at[zq, parity, :, narrow]

    def landed(self, refs, sems):
        for i, ref in enumerate(refs):
            pltpu.make_async_copy(ref, ref, sems.at[i]).wait()

    def remote(self, srcs, dsts, send, recv, device):
        return Both([
            pltpu.make_async_remote_copy(
                src_ref=src, dst_ref=dst, send_sem=send.at[i], recv_sem=recv.at[i],
                device_id=device, device_id_type=MESH,
            ) for i, (src, dst) in enumerate(zip(srcs, dsts))
        ])

    def first(self, index):
        x, z, y, is_me = self.first_target(index == 0)
        wide, narrow = self.rows(x)
        zq, parity, half = lax.rem(self.z, 4), lax.rem(self.y, 2), self.y // 2
        srcs = self.shard.at[wide, 0:256], self.tail.at[narrow]
        dsts = self.main.at[zq, parity, half, wide], self.packed.at[zq, parity, half, narrow]
        far = self.remote(
            srcs, dsts, self.y_send.at[index], self.y_recv.at[half], self.device(x, z, y)
        )
        return is_me, far, srcs, dsts

    def over_y(self):
        for index in range(2):
            is_me, far, srcs, dsts = self.first(index)
            pl.when(self.active & jnp.logical_not(is_me))(far.start)

            @pl.when(self.active & is_me)
            def _():
                for i in range(2):
                    pltpu.make_async_copy(srcs[i], dsts[i], self.local_sems.at[i]).start()

    def second(self, turn, back):
        z, zq, parity = self.from_z(self.order(turn))
        mine = self.piece(zq, parity, self.x)
        return self.remote(
            mine, mine, self.z_send.at[turn, int(back)], self.z_recv.at[z // 2],
            self.device(z=lax.rem(self.z + (7 if back else 1), 8)),
        )

    def seconds(self):
        passive = jnp.logical_not(self.active)
        return (
            (0, True, self.second(0, False)), (0, self.active, self.second(0, True)),
            (1, self.active, self.second(1, False)), (1, passive, self.second(1, True)),
            (2, passive, self.second(2, False)), (2, self.active, self.second(2, True)),
        )

    def over_z(self):
        @pl.when(self.active)
        def _():
            for index in range(2):
                is_me, far, srcs, dsts = self.first(index)
                pl.when(jnp.logical_not(is_me))(far.wait_send)
            for half in range(2):
                is_me = self.first_source(half)[3]
                wide, narrow = self.rows(self.x)
                zq = lax.rem(self.z, 4)
                dst = (
                    self.main.at[zq, self.parity, half, wide],
                    self.packed.at[zq, self.parity, half, narrow],
                )

                @pl.when(is_me)
                def _():
                    self.landed(dst, self.local_sems)

                @pl.when(jnp.logical_not(is_me))
                def _():
                    self.landed(dst, self.y_recv.at[half])

    def from_z(self, index):
        z = 2 * index + self.core
        return z, lax.rem(z, 4), lax.rem(z // 4 + self.y, 2)

    def order(self, turn):
        step = jnp.where(self.active, (0, 6, 2, 4)[turn], (7, 1, 5, 3)[turn])
        return lax.rem(self.z + step, 8) // 2

    def third(self, index, hop):
        z, zq, parity = self.from_z(index)
        owner = self.inner if hop == 2 else self.x
        mine = self.piece(zq, parity, owner)
        return self.remote(
            mine, mine, self.x_send.at[hop, index], self.x_recv.at[owner, index],
            self.device(x=self.outer if hop else self.inner),
        )

    def fourth(self, index, x):
        z, zq, parity = self.from_z(index)
        mine = self.piece(zq, parity, x)
        return self.remote(
            mine, mine, self.c_send.at[x, index], self.c_recv.at[x, index],
            self.device(core=1 - self.core),
        )

    def start_x(self, turn):
        index = self.order(turn)
        z, zq, parity = self.from_z(index)

        @pl.when(z != self.z)
        def _():
            self.landed(self.piece(zq, parity, self.x), self.z_recv.at[index])
        for other, live, copy in self.seconds():
            if other == turn:
                pl.when(live)(copy.start)
        self.third(index, 0).start()
        self.third(index, 1).start()
        self.fourth(index, self.x).start()

    def pass_on(self, x, turn):
        index = self.order(turn)
        z, zq, parity = self.from_z(index)
        self.landed(self.piece(zq, parity, x), self.x_recv.at[x, index])
        if x is self.inner:
            self.third(index, 2).start()
        self.fourth(index, x).start()

    def arrive(self):
        for x in range(4):
            for index in range(4):
                z = 2 * index + 1 - self.core
                other = self.piece(lax.rem(z, 4), lax.rem(z // 4 + self.y, 2), x)
                self.landed(other, self.c_recv.at[x, index])

    def finish(self):
        for turn, live, copy in self.seconds():
            pl.when(live)(copy.wait_send)
        for index in range(4):
            for hop in range(3):
                self.third(index, hop).wait_send()
        for x in range(4):
            for index in range(4):
                self.fourth(index, x).wait_send()


def layer(
    qkv_hbm, tan_hbm, seg_ref, turned_hbm, both_ref,
    qkv_ref, tan_ref, turned_ref, shard_ref, count_ref, in_sems, stage, kv_ref, q_ref, counts_ref, kt_ref, s_ref, st_ref, top_ref, sum_ref, acc_ref, part_ref,
    tail, main, packed, rest, landing, rows_ref, total_ref,
    local_sems, kv_send, kv_recv, q_send, q_recv, n_send, n_recv, f_send,
    y_send, y_recv, z_send, z_recv, x_send, x_recv, c_send, c_recv,
    back_send, back_recv, g_send, g_recv,
):
    ctx, dp, y = lax.axis_index("ctx"), lax.axis_index("dp"), lax.axis_index("head")
    x_lo, z, x_hi, core = ctx // 8, lax.rem(ctx, 8), dp // 2, lax.rem(dp, 2)
    sample = lax.rem(z, 2)
    role = role_of(x_lo, core)
    first, count = work_of(x_lo, z, core)
    weights = Weights(
        shard_ref, tail, main, packed, local_sems.at[pl.ds(4, 2)],
        y_send, y_recv, z_send, z_recv, x_send, x_recv, c_send, c_recv,
    )

    def at(other_x, other_z, other_core):
        return {"ctx": other_x * 8 + other_z, "dp": x_hi * 2 + other_core}

    def is_me(other_x, other_z, other_core):
        return (other_x == x_lo) & (other_z == z) & (other_core == core)

    def remote(src, dst, send, recv, device):
        return pltpu.make_async_remote_copy(
            src_ref=src, dst_ref=dst, send_sem=send, recv_sem=recv, device_id=at(*device),
            device_id_type=MESH,
        )

    def rows_of(block):
        return pl.ds(pl.multiple_of(block * ROWS, ROWS), ROWS)

    loads = [
        pltpu.make_async_copy(src, dst, in_sems.at[i]) for i, (src, dst) in enumerate(
            ((qkv_hbm, qkv_ref), (tan_hbm, tan_ref), (turned_hbm, turned_ref))
        )
    ]
    for load in loads:
        load.start()
    barrier = pltpu.get_barrier_semaphore()
    for other_x in range(2):
        for step in range(8):
            source = (other_x, lax.rem(z + step, 8), sample)
            signal_if(jnp.logical_not(is_me(*source)), barrier, at(*source))
    for mate in ((1 - x_lo, z, core), (x_lo, z, 1 - core), (1 - x_lo, z, 1 - core)):
        signal_if(True, barrier, at(*mate))
    weights.greet(barrier)
    workers = [worker_of(h, ctx, core) for h in range(HEADS)]
    for worker in workers:
        signal_if(jnp.logical_not(is_me(*worker)), barrier, at(*worker))
    for step in range(1, 4):
        signal_if(True, barrier, {"head": lax.rem(y + step, 4)})
    for step in (2, 6):
        signal_if(role == 3, barrier, at(1, lax.rem(z + step, 8), 1))
    own_block = (core == sample) & (first <= ctx) & (ctx < first + count)
    lane = lax.broadcasted_iota(jnp.int32, (8, 128), 1)
    tally = jnp.zeros((8, 128), jnp.int32)
    for v in range(SEGS - 1):
        below = jnp.sum((seg_ref[...] <= v).astype(jnp.int32), axis=1, keepdims=True)
        tally = jnp.where(lane == v, below, tally)
    count_ref[...] = tally
    for load in loads:
        load.wait()
    shard_ref[...] = turned_ref[...].T
    weights.prepare()
    for slot in (4, 5):
        @pl.when(slot >= count)
        def _():
            q_ref[slot * ROWS:(slot + 1) * ROWS] = jnp.zeros((ROWS, 2 * HD), jnp.bfloat16)
    for head in range(HEADS):
        cols = slice(head * HD, (head + 1) * HD)
        stage[head, 0, :, 0:HD] = qkv_ref[1, :, cols]
        stage[head, 0, :, HD:] = tan_ref[1, :, cols]
        stage[head, 1, :, 0:HD] = qkv_ref[2, :, cols]
        stage[head, 1, :, HD:] = tan_ref[2, :, cols]
        stage[head, 2, :, 0:HD] = tan_ref[0, :, cols]
        stage[head, 2, :, HD:] = qkv_ref[0, :, cols]
    pl.semaphore_wait(
        barrier,
        22 - (core == sample).astype(jnp.int32) + weights.greetings()
        + count - own_block.astype(jnp.int32) + 2 * (role == 3).astype(jnp.int32),
    )
    weights.over_y()

    sends = []

    def send(device, src, dst, send_sem, recv_sem, local_sem, live=True):
        mine = is_me(*device)
        far = remote(src, dst, send_sem, recv_sem, device)
        away = live & jnp.logical_not(mine)
        pl.when(away)(far.start)

        @pl.when(mine)
        def _():
            pltpu.make_async_copy(src, dst, local_sem).start()
        sends.append((away, far))

    for other_x in range(2):
        for step in range(4):
            device = (other_x, 2 * lax.rem(z // 2 + step, 4) + core)
            for other_core in range(2):
                send(
                    device + (other_core,), count_ref, counts_ref.at[ctx],
                    n_send.at[other_x, step, other_core], n_recv.at[ctx], local_sems.at[0],
                )
    for head in range(HEADS):
        slot = lax.rem(ctx, 4) if head == 4 else ctx - chunk_start(chunk_of(ctx))
        send(
            worker_of(head, ctx, core), stage.at[head, 2], q_ref.at[rows_of(slot)],
            q_send.at[head], q_recv.at[slot], local_sems.at[2],
        )
    weights.over_z()
    def send_keys(step):
        turn = lax.rem(z // 2 + (0, 1, 3, 2)[step], 4)
        slice_z = 2 * turn + core
        send(
            (x_lo, slice_z, jnp.where(x_lo == 0, core, 0)), stage.at[turn, 0:2],
            kv_ref.at[:, rows_of(ctx)], kv_send.at[0, step], kv_recv.at[ctx], local_sems.at[1],
        )
        steps = lax.rem(slice_z - z + 8, 8)
        send(
            (1, slice_z, 1), stage.at[HEADS - 1, 0:2], kv_ref.at[:, rows_of(ctx)],
            kv_send.at[1, step], kv_recv.at[ctx], local_sems.at[1], (steps <= 2) | (steps >= 6),
        )

    entry = (x_lo == 0) & (core == sample)
    third = role == 2

    def forward(block, mate, index):
        dst = kv_ref.at[:, rows_of(block)]
        return remote(dst, dst, f_send.at[block, index], kv_recv.at[block], mate)

    def forwards(direct, block):
        to_core = (entry, forward(block, (0, z, 1 - core), 0))
        if direct:
            to_x = forward(block, (1 - x_lo, z, jnp.where(entry, 0, sample)), 1)
            return [to_core, (entry | third, to_x)]
        return [to_core]

    def arrived(block, ref, own_sem, sem):
        mine = (block == ctx) & (core == sample)

        @pl.when(mine)
        def _():
            pltpu.make_async_copy(ref, ref, own_sem).wait()

        @pl.when(jnp.logical_not(mine))
        def _():
            pltpu.make_async_copy(ref, ref, sem).wait()

    chain = {6: 2, 7: 2, 1: 6}

    def on(block, step):
        dst = kv_ref.at[:, rows_of(block)]
        return remote(
            dst, dst, f_send.at[block, 0], kv_recv.at[block], (1, lax.rem(z + chain[step], 8), 1)
        )

    def pass_keys(direct, step):
        block = (x_lo if direct else 1 - x_lo) * 8 + lax.rem(z + step, 8)

        @pl.when(role != 3)
        def _():
            arrived(block, kv_ref.at[:, rows_of(block)], local_sems.at[1], kv_recv.at[block])
            for live, copy in forwards(direct, block):
                pl.when(live)(copy.start)

        if direct:
            @pl.when(role == 3)
            def _():
                for other_x in range(2):
                    block = other_x * 8 + lax.rem(z + step, 8)
                    ref = kv_ref.at[:, rows_of(block)]
                    arrived(block, ref, local_sems.at[1], kv_recv.at[block])
                    if step in chain:
                        on(block, step).start()

    near = (0, 1, 7, 2, 6, 3, 5, 4)

    def events(order):
        for kind, turn in order:
            if kind in "DR":
                pass_keys(kind == "D", near[turn])
            elif kind == "X":
                weights.start_x(turn)
            elif kind == "K":
                send_keys(turn)
            else:
                x = {"I": weights.inner, "O": weights.outer, "F": weights.far}[kind]
                weights.pass_on(x, turn)

    events(ORDERS[0])
    for direct in (True, False):
        for step in range(8):
            block = (x_lo if direct else 1 - x_lo) * 8 + lax.rem(z + step, 8)
            arrived(block, counts_ref.at[block], local_sems.at[0], n_recv.at[block])
    for slot in range(SLOTS):
        @pl.when(slot < count)
        def _():
            arrived(first + slot, q_ref.at[rows_of(slot)], local_sems.at[2], q_recv.at[slot])

    def back(slot):
        block = lax.min(first + slot, BLOCKS - 1)
        head = jnp.where(role == 3, HEADS - 1, z // 2)
        own = (block == ctx) & (core == sample)
        dst = landing.at[y, head]
        far = pltpu.make_async_remote_copy(
            src_ref=part_ref.at[slot], dst_ref=dst, send_sem=back_send.at[slot],
            recv_sem=back_recv.at[head], device_id={"ctx": block, "dp": x_hi * 2 + sample},
            device_id_type=MESH,
        )
        return (slot < count) & own, (slot < count) & jnp.logical_not(own), far, dst

    scale = 1.0 / math.sqrt(HD)
    power = scale / math.log(2.0)
    below = jnp.sum(counts_ref[...], axis=0)
    bounds = [below[0:1, v:v + 1] for v in range(SEGS - 1)]

    def of_position(position, values):
        result = values[SEGS - 1]
        for v in range(SEGS - 2, -1, -1):
            result = jnp.where(position < bounds[v], values[v], result)
        return result

    starts = [jnp.zeros((1, 1), jnp.int32)] + bounds
    ends = bounds + [jnp.full((1, 1), SEQ, jnp.int32)]

    @pl.loop(0, KTILES)
    def _(tile):
        keys = pl.ds(pl.multiple_of(tile * TILE, TILE), TILE)
        kt_ref[tile] = kv_ref[0, keys].T

    for part in range(2):
        position = (first + 3 * part) * ROWS + lax.broadcasted_iota(jnp.int32, (PART, 1), 0)
        start = of_position(position, starts)
        end = of_position(position, ends)
        column = lax.broadcasted_iota(jnp.int32, (1, TILE), 1)
        rows = slice(part * PART, (part + 1) * PART)
        top_ref[...] = jnp.full_like(top_ref, -1e30)
        sum_ref[...] = jnp.zeros_like(sum_ref)
        acc_ref[...] = jnp.zeros_like(acc_ref)

        @pl.loop(0, KTILES)
        def _(tile):
            s = jnp.dot(
                q_ref[rows, HD:], kt_ref[tile, 0:HD], preferred_element_type=jnp.float32
            )
            place = column + tile * TILE
            s = jnp.where((place >= start) & (place < end), s, -1e30)
            s_ref[tile] = s
            st_ref[tile] = jnp.dot(
                q_ref[rows, :], kt_ref[tile], preferred_element_type=jnp.float32
            )
            top_ref[...] = jnp.maximum(top_ref[...], fold(jnp.maximum, s))

        top = jnp.max(top_ref[...], axis=1, keepdims=True)

        @pl.loop(0, KTILES)
        def _(tile):
            keys = pl.ds(pl.multiple_of(tile * TILE, TILE), TILE)
            prob = jnp.exp2((s_ref[tile] - top) * power)
            weighted = prob * st_ref[tile]
            sum_ref[0] += fold(jnp.add, prob)
            sum_ref[1] += fold(jnp.add, weighted)
            acc_ref[:, 0:2 * HD] += jnp.dot(
                prob.astype(jnp.bfloat16), kv_ref[1, keys], preferred_element_type=jnp.float32
            )
            acc_ref[:, 2 * HD:] += jnp.dot(
                weighted.astype(jnp.bfloat16), kv_ref[1, keys, 0:HD],
                preferred_element_type=jnp.float32,
            )

        inverse = 1.0 / jnp.sum(sum_ref[0], axis=1, keepdims=True)
        drift = jnp.sum(sum_ref[1], axis=1, keepdims=True) * scale
        plain = acc_ref[:, 0:HD] * inverse
        turned = (acc_ref[:, HD:2 * HD] + acc_ref[:, 2 * HD:] * scale - drift * plain) * inverse
        for slot in range(3):
            piece = slice(slot * ROWS, (slot + 1) * ROWS)
            part_ref[part * 3 + slot, 0] = plain[piece].astype(jnp.bfloat16)
            part_ref[part * 3 + slot, 1] = turned[piece].astype(jnp.bfloat16)
        for slot in range(part * 3, part * 3 + 3):
            own, live, far, dst = back(slot)
            pl.when(live)(far.start)

            @pl.when(own)
            def _():
                pltpu.make_async_copy(part_ref.at[slot], dst, local_sems.at[3]).start()
        events(ORDERS[1 + part])

    def to_y(owner, h, step, index):
        piece = landing.at[owner, h]
        return pltpu.make_async_remote_copy(
            src_ref=piece, dst_ref=piece, send_sem=g_send.at[h, index],
            recv_sem=g_recv.at[owner, h], device_id={"head": lax.rem(y + step, 4)}, device_id_type=MESH,
        )

    def gathers(h):
        owner, step = (3, 1) if h < 3 else (1, 3)
        return (
            to_y(y, h, 1, 0), to_y(y, h, 3, 1), to_y(lax.rem(y + owner, 4), h, step, 2),
        )

    for h in range(HEADS):
        mine = is_me(*workers[h])

        @pl.when(mine)
        def _():
            pltpu.make_async_copy(part_ref.at[0], landing.at[y, h], local_sems.at[3]).wait()

        @pl.when(jnp.logical_not(mine))
        def _():
            pltpu.make_async_copy(part_ref.at[0], landing.at[y, h], back_recv.at[h]).wait()
        for copy in gathers(h)[0:2]:
            copy.start()

    events(ORDERS[3])
    weights.arrive()
    for zq in range(4):
        for parity in range(2):
            for half in range(2):
                for quarter in range(4):
                    for side in range(2):
                        row = quarter * 160 + side * 80
                        rest[parity, half, row:row + 80, zq * 64:(zq + 1) * 64] = packed[
                            zq, parity, half, quarter * 80:(quarter + 1) * 80, side * 64:(side + 1) * 64
                        ]

    def gathered(step, h):
        other = lax.rem(y + step, 4)
        pltpu.make_async_copy(part_ref.at[0], landing.at[other, h], g_recv.at[other, h]).wait()

    for turn, step in enumerate((0, 1, 3, 2)):
        other = lax.rem(y + step, 4)
        if turn == 1:
            for h in range(HEADS):
                gathered(1, h)
                if h < 3:
                    gathered(3, h)
                gathers(h)[2].start()
        for h in range(HEADS):
            if step == 2 or (step == 3 and h >= 3):
                gathered(step, h)
            for kind in range(2):
                rows_ref[kind * ROWS:(kind + 1) * ROWS, h * HD:(h + 1) * HD] = landing[other, h, kind]
        parity, half = lax.rem(other, 2), other // 2
        for zq in range(5):
            weight = main[zq, parity, half] if zq < 4 else rest[parity, half]
            term = jnp.dot(rows_ref[...], weight, preferred_element_type=jnp.float32)
            total_ref[zq] = term if turn == 0 else total_ref[zq] + term

    for zq in range(4):
        for kind in range(2):
            rows = slice(kind * ROWS, (kind + 1) * ROWS)
            both_ref[kind, :, zq * 320:zq * 320 + 256] = total_ref[zq, rows].astype(jnp.bfloat16)
            both_ref[kind, :, zq * 320 + 256:(zq + 1) * 320] = (
                total_ref[4, rows, zq * 64:(zq + 1) * 64].astype(jnp.bfloat16)
            )

    for direct in (True, False):
        for step in range(8):
            block = (x_lo if direct else 1 - x_lo) * 8 + lax.rem(z + step, 8)
            for live, copy in forwards(direct, block):
                pl.when(live)(copy.wait_send)
    @pl.when(role == 3)
    def _():
        for step in chain:
            for other_x in range(2):
                on(other_x * 8 + lax.rem(z + step, 8), step).wait_send()
    for live, copy in sends:
        pl.when(live)(copy.wait_send)
    for slot in range(SLOTS):
        own, live, far, dst = back(slot)
        pl.when(live)(far.wait_send)
    for h in range(HEADS):
        for copy in gathers(h):
            copy.wait_send()
    weights.finish()


def local(qkv, tangent, segments, out_weight):
    vmem = pl.BlockSpec(memory_space=pltpu.VMEM)
    dma = pltpu.SemaphoreType.DMA
    bf16, f32 = jnp.bfloat16, jnp.float32
    hbm = pl.BlockSpec(memory_space=pl.ANY)
    both = pl.pallas_call(
        layer,
        out_shape=jax.ShapeDtypeStruct((2, ROWS, 1280), bf16),
        in_specs=[hbm, hbm, vmem, hbm],
        out_specs=vmem,
        scratch_shapes=[
            pltpu.VMEM((3, ROWS, HEADS * HD), bf16),
            pltpu.VMEM((3, ROWS, HEADS * HD), bf16),
            pltpu.VMEM((320, 640), bf16),
            pltpu.VMEM((640, 320), bf16),
            pltpu.VMEM((8, 128), jnp.int32),
            dma((3,)),
            pltpu.VMEM((HEADS, 3, ROWS, 2 * HD), bf16),
            pltpu.VMEM((2, SEQ, 2 * HD), bf16),
            pltpu.VMEM((SLOTS * ROWS, 2 * HD), bf16),
            pltpu.VMEM((BLOCKS, 8, 128), jnp.int32),
            pltpu.VMEM((KTILES, 2 * HD, TILE), bf16),
            pltpu.VMEM((KTILES, PART, TILE), f32),
            pltpu.VMEM((KTILES, PART, TILE), f32),
            pltpu.VMEM((PART, 128), f32),
            pltpu.VMEM((2, PART, 128), f32),
            pltpu.VMEM((PART, 3 * HD), f32),
            pltpu.VMEM((SLOTS, 2, ROWS, HD), bf16),
            pltpu.VMEM((320, 128), bf16),
            pltpu.VMEM((4, 2, 2, 640, 256), bf16),
            pltpu.VMEM((4, 2, 2, 320, 128), bf16),
            pltpu.VMEM((2, 2, 640, 256), bf16),
            pltpu.VMEM((4, HEADS, 2, ROWS, HD), bf16),
            pltpu.VMEM((2 * ROWS, HEADS * HD), bf16),
            pltpu.VMEM((5, 2 * ROWS, 256), f32),
            dma((6,)), dma((2, 4)), dma((BLOCKS,)), dma((HEADS,)), dma((SLOTS,)),
            dma((2, 4, 2)), dma((BLOCKS,)), dma((BLOCKS, 2)),
            dma((2, 2)), dma((2, 2)), dma((3, 2, 2)), dma((4, 2)),
            dma((3, 4, 2)), dma((4, 4, 2)), dma((4, 4, 2)), dma((4, 4, 2)),
            dma((SLOTS,)), dma((HEADS,)), dma((HEADS, 3)), dma((4, HEADS)),
        ],
        compiler_params=pltpu.CompilerParams(
            collective_id=0, has_side_effects=True, vmem_limit_bytes=56 * 2**20
        ),
        name="layer",
    )(qkv, tangent, segments.reshape(1, ROWS), out_weight.T)
    return both[0], both[1]


def solution(mesh):
    return jax.shard_map(
        local,
        mesh=mesh,
        in_specs=(
            P(None, ("dp", "ctx"), "head"),
            P(None, ("dp", "ctx"), "head"),
            P(("dp", "ctx")),
            P("head", "ctx"),
        ),
        out_specs=(P(("dp", "ctx"), "head"), P(("dp", "ctx"), "head")),
        check_vma=False,
    )
```

profile of v0, /device:TPU:1, one launch (start us, length us, event | category | flops | bytes accessed | tf_op | source)
XLA Modules:
  0.0 119.3 jit_solution(1734534807177616706)
XLA Ops:
  0.6 116.5 %layer.1 = bf16[2,160,1280]{2,1,0:T(8,128)(2,1)} custom-call(bf16[3,160,640]{2,1,0:T(8,128)(2,1)} %qkv_hbm.1, bf16[3,160,640]{2,1,0:T(8,128)(2,1)} %tan_hbm.1, s32[1,160]{1,0:T(1,128)} %bitcast.7, bf16[320,640]{1,0:T(8,128)(2,1)} %bitcast.6), custom_call_target="tpu_custom_call" | custom-call | tf_op jit(solution)/shard_map/layer/pallas_call | solution.py:683
  117.2 2.1 %slice_bitcast_fusion = (bf16[160,1280]{1,0:T(8,128)(2,1)}, bf16[160,1280]{1,0:T(8,128)(2,1)}) fusion(bf16[2,160,1280]{2,1,0:T(8,128)(2,1)} %layer.1), kind=kLoop, calls=%fused_computation | loop fusion | bytes 1638400 | tf_op jit(solution)/shard_map/squeeze | solution.py:724
where the time goes:
time: 119 us
  Pallas kernels  117 us (98%)
  local copies, waits for them, and re-layouts  2.07 us (2%)
    pallas_call x1, Pallas kernels, local(): pl.pallas_call(layer, out_shape=jax.ShapeDtypeStruct((2, ROWS, 1280), bf1...  117 us

commit v1 on v0

--- a/solution.py
+++ b/solution.py
@@ -27,8 +27,8 @@
     several("X", 0, 1) + several("K", 0, 2) + several("X", 1, 3) + several("K", 2, 4) + several("D", 0, 2)
     + several("X", 3, 4) + several("D", 2, 5) + several("I", 0, 4) + several("D", 5, 8) + several("R", 0, 8),
     several("O", 0, 4),
+    [],
     several("F", 0, 4),
-    [],
 )
 KTILES = SEQ // TILE
 MESH = pl.DeviceIdType.MESH

time: 119 us -> 121 us (1.017); the launches traced: 119 us -> 119 us
  no operation moved by 1% of the time
where the time goes in v1:
time: 121 us; the launch traced here: 119 us
  Pallas kernels  116 us (96%)
  local copies, waits for them, and re-layouts  2.07 us (2%)
    pallas_call x1, Pallas kernels, local(): pl.pallas_call(layer, out_shape=jax.ShapeDtypeStruct((2, ROWS, 1280), bf1...  116 us

profile of v1, /device:TPU:1, one launch (start us, length us, event | category | flops | bytes accessed | tf_op | source)
XLA Modules:
  0.0 119.2 jit_solution(4636959359632514449)
XLA Ops:
  0.6 116.5 %layer.1 = bf16[2,160,1280]{2,1,0:T(8,128)(2,1)} custom-call(bf16[3,160,640]{2,1,0:T(8,128)(2,1)} %qkv_hbm.1, bf16[3,160,640]{2,1,0:T(8,128)(2,1)} %tan_hbm.1, s32[1,160]{1,0:T(1,128)} %bitcast.7, bf16[320,640]{1,0:T(8,128)(2,1)} %bitcast.6), custom_call_target="tpu_custom_call" | custom-call | tf_op jit(solution)/shard_map/layer/pallas_call | solution.py:683
  117.1 2.1 %slice_bitcast_fusion = (bf16[160,1280]{1,0:T(8,128)(2,1)}, bf16[160,1280]{1,0:T(8,128)(2,1)}) fusion(bf16[2,160,1280]{2,1,0:T(8,128)(2,1)} %layer.1), kind=kLoop, calls=%fused_computation | loop fusion | bytes 1638400 | tf_op jit(solution)/shard_map/squeeze | solution.py:724
